TPU v7x, 32 devices: a whole 2x2x4 slice. The times are simulated.
32 devices in a mesh: row: 4 (over y, core), col: 8 (over z, x).
Axes of the slice: x: 2, y: 2, z: 4, core: 2. Of those that a mesh axis runs over, the one named last changes fastest.
Arguments:
- density: float32 [4, 8, 7, 2, 128, 128], P('row', 'col'), may hold values from -1 to 2, as said below
- hamiltonian: float32 [4, 8, 7, 2, 128, 128], P('row', 'col'), may hold values from -2 to 4, as said below
- offsets: int32 [7, 3], replicated, may hold values from -1 to 1, as said below
- branch: int32 [3], replicated, may hold values from 0 to 1, as said below
Outputs:
- new_density: float32 [4, 8, 7, 2, 128, 128], P('row', 'col')
- grad_density: float32 [4, 8, 7, 2, 128, 128], P('row', 'col')
- totals: float32 [2], replicated
Inputs may be any that keep to these rules, and one draw needn't show every extreme that they name: 7 distinct offsets; (0, 0, 0) is one of them and with each offset its negative (layer step modulo 2) is another; row and column steps lie in -1 to 1, and nonzero row steps and nonzero column steps both occur. `branch`: each entry is 0 or 1, and not all entries are equal. `density`: the matrix is symmetric: entry [p, q, t, s] is the transpose of the entry of the opposite offset at the transposed block position. `hamiltonian`: the matrix is symmetric, in the same sense as the density.
All inputs are finite; a program needn't handle non-finite values.
Results may differ from a plain program's by a relative error of at most 0.0003.
Values sent between devices are 32-bit elements; how exact they have to be, the bound alone decides.
No kernel may reach another device: no remote copies, remote signals or barrier semaphores. Data moves between devices by JAX's collectives and lax.ppermute only.
A program may use at most 128 MiB of HBM per device.

v0:
```python
import jax
import jax.numpy as jnp
from jax import lax
from jax.sharding import PartitionSpec as P

FULL_PRECISION = lax.Precision.HIGHEST


def with_halo(block, sides, width):
    for axis, dim in sides:
        count = lax.axis_size(axis)
        forward = [(i, i + 1) for i in range(count - 1)]
        forward.append((count - 1, 0))
        backward = [(target, source) for source, target in forward]
        low = lax.ppermute(
            lax.slice_in_dim(block, block.shape[dim] - width, None, axis=dim), axis, forward
        )
        high = lax.ppermute(lax.slice_in_dim(block, 0, width, axis=dim), axis, backward)
        block = jnp.concatenate([low, block, high], axis=dim)
    return block


def pair_tables(offsets, row_count, col_count, layer_count):
    moduli = jnp.array([row_count, col_count, layer_count], jnp.int32)
    summed = offsets[:, None, :] + offsets[None, :, :]
    differ = summed[None, :, :, :] - offsets[:, None, None, :]
    matches = jnp.all(differ % moduli == 0, axis=-1).astype(jnp.int32)
    partner = jnp.argmax(matches, axis=2)
    usable = jnp.max(matches, axis=2)
    return (partner, usable)


def sparse_product(left_rim, right_rim, offsets, partner, usable):
    count_offsets = offsets.shape[0]
    layer_count = left_rim.shape[2]
    col_pick = 1 - offsets[:, 1]
    row_pick = 1 + offsets[:, 0]
    layer_pick = (jnp.arange(layer_count, dtype=jnp.int32)[None, :] + offsets[:, 2:3]) % layer_count
    left_slots = jnp.arange(count_offsets, dtype=jnp.int32)

    def one_target(target):
        partners_row = partner[target]
        keep_mask = usable[target].astype(jnp.float32)
        left_part = left_rim[col_pick[partners_row], left_slots] * keep_mask[:, None, None, None]
        right_part = right_rim[row_pick[:, None], partners_row[:, None], layer_pick]
        return jnp.einsum("tsab,tsbc->sac", left_part, right_part, precision=FULL_PRECISION)

    return lax.map(one_target, jnp.arange(count_offsets, dtype=jnp.int32))


def iterate_rims(field):
    rows_rim = with_halo(field, (("row", 0),), 1)[:, 0]
    cols_rim = with_halo(field, (("col", 1),), 1)[0]
    return (cols_rim, rows_rim)


def outer_rims(field):
    rows_rim = with_halo(field, (("row", 0),), 1)[:, 0]
    cols_rim = with_halo(field, (("col", 1),), 1)[0]
    return (cols_rim, rows_rim)


def local(density, hamiltonian, offsets, branch):
    row_count = lax.axis_size("row")
    col_count = lax.axis_size("col")
    step_count = branch.shape[0]
    layer_count = density.shape[3]
    block_size = density.shape[4]
    matrix_order = block_size * layer_count * row_count * col_count
    partner, usable = pair_tables(offsets, row_count, col_count, layer_count)
    zero_slot = jnp.all(offsets == 0, axis=1).astype(jnp.float32)
    identity_part = zero_slot[:, None, None, None] * jnp.eye(block_size, dtype=jnp.float32)
    branch_signs = (2 * branch - 1).astype(jnp.float32)
    density_rows = with_halo(density, (("row", 0),), 1)[:, 0]
    density_cols = with_halo(density, (("col", 1),), 1)[0]
    density_rims = (density_cols, density_rows)
    iterates = [density]
    rims = [density_rims]
    for step in range(step_count):
        current = iterates[-1]
        square = sparse_product(rims[-1][0], rims[-1][1], offsets, partner, usable)[None, None]
        following = current + branch_signs[step] * (current - square)
        iterates.append(following)
        if step + 1 < step_count:
            rims.append(iterate_rims(following))
    new_density = iterates[-1]
    global_sums = lax.psum(
        (jnp.sum(hamiltonian * new_density), jnp.sum(new_density * identity_part)), ("row", "col")
    )
    totals = jnp.stack(global_sums) / matrix_order
    excess = totals[1] - 0.5
    outer_grad = hamiltonian + excess * identity_part
    last = step_count - 1
    last_cols, last_rows = rims[last]
    cotangent_rows = with_halo(outer_grad, (("row", 0),), 1)[:, 0]
    cotangent_cols = with_halo(outer_grad, (("col", 1),), 1)[0]
    cross_terms = sparse_product(
        cotangent_cols, last_rows, offsets, partner, usable
    ) + sparse_product(last_cols, cotangent_rows, offsets, partner, usable)
    cross_terms = cross_terms[None, None]
    outer_grad = (1.0 + branch_signs[last]) * outer_grad - branch_signs[last] * cross_terms
    for step in range(last - 1, -1, -1):
        grad_cols, grad_rows = outer_rims(outer_grad)
        step_cols, step_rows = rims[step]
        cross_terms = sparse_product(
            grad_cols, step_rows, offsets, partner, usable
        ) + sparse_product(step_cols, grad_rows, offsets, partner, usable)
        outer_grad = (1.0 + branch_signs[step]) * outer_grad - branch_signs[step] * cross_terms[
            None, None
        ]
    return (new_density, outer_grad, totals)


def solution(mesh):
    return jax.shard_map(
        local,
        mesh=mesh,
        in_specs=(
            P("row", "col", None, None, None, None),
            P("row", "col", None, None, None, None),
            P(),
            P(),
        ),
        out_specs=(
            P("row", "col", None, None, None, None),
            P("row", "col", None, None, None, None),
            P(),
        ),
        check_vma=False,
    )
```

profile of v0, /device:TPU:0, one launch (start us, length us, event | category | flops | bytes accessed | tf_op | source)
XLA Modules:
  0.0 907.2 jit_solution(11616821854511259699)
XLA Ops:
  14.9 6.7 collective-permute-done.2
  24.1 3.4 maximum_bitcast_fusion.1
  27.6 17.5 %collective-permute-done = f32[1,1,7,2,128,128]{5,4,3,2,1,0:T(8,128)S(1)} collective-permute-done((f32[1,1,7,2,128,128]{5,4,3,2,1,0:T(8,128)}, f32[1,1,7,2,128,128]{5,4,3,2,1,0:T(8,128)S(1)}, u32[]{:S(2)}, u32[]{:S(2)}) %collective-permute-start) | collective-permute-done | bytes 917536 | tf_op jit(solution)/shard_map/ppermute | solution.py:15
  51.4 70.1 %while.117 = (s32[]{:T(128)}, f32[7,2,128,128]{3,2,1,0:T(8,128)}, s32[7]{0:T(128)S(1)}, s32[7,7]{1,0:T(8,128)S(1)}, s32[7]{0:T(128)S(1)}, /*index=5*/f32[3,7,2,1...) while((s32[]{:T(128)}, f32[7,2,128,128]{3,2,1,0:T(8,128)}, ...), condition=%wide.region_4.5_spmd.clone.clone, body=%wide.region_3.4_spmd.clone.clone.sunk | while | flops 352552384 | bytes 5641867 | solution.py:48
  125.4 4.5 collective-permute-start.5
  129.9 15.4 %collective-permute-done.6 = f32[1,1,7,2,128,128]{5,4,3,2,1,0:T(8,128)S(1)} collective-permute-done((f32[1,1,7,2,128,128]{5,4,3,2,1,0:T(8,128)S(1)}, f32[1,1,7,2,128,128]{5,4,3,2,1,0:T(8,128)S(1)}, u32[]{:S(2)}, u32[]{:S(2)}) %collective-permute-start.6) | collective-permute-done | bytes 917536 | tf_op jit(solution)/shard_map/ppermute | solution.py:15
  148.4 15.4 %collective-permute-done.4 = f32[1,1,7,2,128,128]{5,4,3,2,1,0:T(8,128)S(1)} collective-permute-done((f32[1,1,7,2,128,128]{5,4,3,2,1,0:T(8,128)S(1)}, f32[1,1,7,2,128,128]{5,4,3,2,1,0:T(8,128)S(1)}, u32[]{:S(2)}, u32[]{:S(2)}) %collective-permute-start.4) | collective-permute-done | bytes 917536 | tf_op jit(solution)/shard_map/ppermute | solution.py:15
  170.0 65.7 %while.118 = (s32[]{:T(128)}, f32[7,2,128,128]{3,2,1,0:T(8,128)S(1)}, s32[7]{0:T(128)S(1)}, s32[7,7]{1,0:T(8,128)S(1)}, s32[7]{0:T(128)S(1)}, /*index=5*/f32[3,7...) while((s32[]{:T(128)}, ...), condition=%wide.region_6.7_spmd.clone.clone, body=%wide.region_5.6_spmd.clone.clone.sunk | while | flops 352552384 | bytes 5641843 | solution.py:48
  240.7 4.7 collective-permute-start.9
  245.5 14.1 %collective-permute-done.10 = f32[1,1,7,2,128,128]{5,4,3,2,1,0:T(8,128)S(1)} collective-permute-done((f32[1,1,7,2,128,128]{5,4,3,2,1,0:T(8,128)S(1)}, f32[1,1,7,2,128,128]{5,4,3,2,1,0:T(8,128)S(1)}, u32[]{:S(2)}, u32[]{:S(2)}) %collective-permute-start.10) | collective-permute-done | bytes 917536 | tf_op jit(solution)/shard_map/ppermute | solution.py:15
  260.6 3.2 maximum_bitcast_fusion.5
  263.8 16.5 %collective-permute-done.8 = f32[1,1,7,2,128,128]{5,4,3,2,1,0:T(8,128)S(1)} collective-permute-done((f32[1,1,7,2,128,128]{5,4,3,2,1,0:T(8,128)S(1)}, f32[1,1,7,2,128,128]{5,4,3,2,1,0:T(8,128)S(1)}, u32[]{:S(2)}, u32[]{:S(2)}) %collective-permute-start.8) | collective-permute-done | bytes 917536 | tf_op jit(solution)/shard_map/ppermute | solution.py:15
  280.3 3.2 collective-permute-done.9
  287.6 70.1 %while.119 = (s32[]{:T(128)}, f32[7,2,128,128]{3,2,1,0:T(8,128)}, s32[7]{0:T(128)S(1)}, s32[7,7]{1,0:T(8,128)S(1)}, s32[7]{0:T(128)S(1)}, /*index=5*/f32[3,7,2,1...) while((s32[]{:T(128)}, f32[7,2,128,128]{3,2,1,0:T(8,128)}, ...), condition=%wide.region_8.9_spmd.clone.clone, body=%wide.region_7.8_spmd.clone.clone.sunk | while | flops 352552384 | bytes 5641867 | solution.py:48
  357.7 4.0 multiply_reduce_fusion.1
  361.7 39.5 %all-reduce = (f32[1]{0:T(128)}, f32[1]{0:T(128)}) all-reduce(f32[1]{0:T(128)} %bitcast.19, f32[1]{0:T(128)} %bitcast.18), channel_id=1, replica_groups=mesh['row'=4,'col'=8] {'row','col'}, use_global_device_ids=true, to_apply=%region_13.14 | all-reduce | flops 2 | bytes 16 | tf_op jit(solution)/shard_map/psum | solution.py:87
  411.2 12.7 %collective-permute-done.14 = f32[1,1,7,2,128,128]{5,4,3,2,1,0:T(8,128)S(1)} collective-permute-done((f32[1,1,7,2,128,128]{5,4,3,2,1,0:T(8,128)S(1)}, f32[1,1,7,2,128,128]{5,4,3,2,1,0:T(8,128)S(1)}, u32[]{:S(2)}, u32[]{:S(2)}) %collective-permute-start.14) | collective-permute-done | bytes 917536 | tf_op jit(solution)/shard_map/ppermute | solution.py:15
  429.2 68.2 %while.121 = (s32[]{:T(128)}, f32[7,2,128,128]{3,2,1,0:T(8,128)}, s32[7]{0:T(128)S(1)}, s32[7,7]{1,0:T(8,128)S(1)}, s32[7]{0:T(128)S(1)}, /*index=5*/f32[3,7,2,1...) while((s32[]{:T(128)}, f32[7,2,128,128]{3,2,1,0:T(8,128)}, ...), condition=%wide.region_17.18_spmd.clone.clone, body=%wide.region_16.17_spmd.clone.clone.sunk | while | flops 352552384 | bytes 5641867 | solution.py:48
  497.4 3.4 maximum_bitcast_fusion.6
  500.9 67.1 %while.120 = (s32[]{:T(128)}, f32[7,2,128,128]{3,2,1,0:T(8,128)S(1)}, s32[7]{0:T(128)S(1)}, s32[7,7]{1,0:T(8,128)S(1)}, s32[7]{0:T(128)S(1)}, /*index=5*/f32[3,7...) while((s32[]{:T(128)}, ...), condition=%wide.region_15.16_spmd.clone.clone, body=%wide.region_14.15_spmd.clone.clone.sunk | while | flops 352552384 | bytes 5641843 | solution.py:48
  575.7 3.7 collective-permute-start.17
  579.4 13.0 %collective-permute-done.18 = f32[1,1,7,2,128,128]{5,4,3,2,1,0:T(8,128)S(1)} collective-permute-done((f32[1,1,7,2,128,128]{5,4,3,2,1,0:T(8,128)S(1)}, f32[1,1,7,2,128,128]{5,4,3,2,1,0:T(8,128)S(1)}, u32[]{:S(2)}, u32[]{:S(2)}) %collective-permute-start.18) | collective-permute-done | bytes 917536 | tf_op jit(solution)/shard_map/ppermute | solution.py:15
  597.3 69.6 %while.123 = (s32[]{:T(128)}, f32[7,2,128,128]{3,2,1,0:T(8,128)}, s32[7]{0:T(128)S(1)}, s32[7,7]{1,0:T(8,128)S(1)}, s32[7]{0:T(128)S(1)}, /*index=5*/f32[3,7,2,1...) while((s32[]{:T(128)}, f32[7,2,128,128]{3,2,1,0:T(8,128)}, ...), condition=%wide.region_21.22_spmd.clone.clone, body=%wide.region_20.21_spmd.clone.clone.sunk | while | flops 352552384 | bytes 5641867 | solution.py:48
  666.9 3.5 maximum_bitcast_fusion.8
  671.3 69.6 %while.122 = (s32[]{:T(128)}, f32[7,2,128,128]{3,2,1,0:T(8,128)}, s32[7]{0:T(128)S(1)}, s32[7,7]{1,0:T(8,128)S(1)}, s32[7]{0:T(128)S(1)}, /*index=5*/f32[3,7,2,1...) while((s32[]{:T(128)}, f32[7,2,128,128]{3,2,1,0:T(8,128)}, ...), condition=%wide.region_19.20_spmd.clone.clone, body=%wide.region_18.19_spmd.clone.clone.sunk | while | flops 352552384 | bytes 5641867 | solution.py:48
  740.9 3.3 bitcast_subtract_fusion.1
  747.2 4.7 collective-permute-start.21
  751.8 13.8 %collective-permute-done.22 = f32[1,1,7,2,128,128]{5,4,3,2,1,0:T(8,128)S(1)} collective-permute-done((f32[1,1,7,2,128,128]{5,4,3,2,1,0:T(8,128)}, f32[1,1,7,2,128,128]{5,4,3,2,1,0:T(8,128)S(1)}, u32[]{:S(2)}, u32[]{:S(2)}) %collective-permute-start.22) | collective-permute-done | bytes 917536 | tf_op jit(solution)/shard_map/ppermute | solution.py:15
  770.0 64.2 %while.125 = (s32[]{:T(128)}, f32[7,2,128,128]{3,2,1,0:T(8,128)S(1)}, s32[7]{0:T(128)S(1)}, s32[7,7]{1,0:T(8,128)S(1)}, s32[7]{0:T(128)S(1)}, /*index=5*/f32[3,7...) while((s32[]{:T(128)}, ...), condition=%wide.region_25.26_spmd.clone.clone, body=%wide.region_24.25_spmd.clone.clone.sunk | while | flops 352552384 | bytes 5641843 | solution.py:48
  834.3 3.9 maximum_bitcast_fusion.10
  838.3 65.6 %while.124 = (s32[]{:T(128)}, f32[7,2,128,128]{3,2,1,0:T(8,128)S(1)}, s32[7]{0:T(128)S(1)}, s32[7,7]{1,0:T(8,128)S(1)}, s32[7]{0:T(128)S(1)}, /*index=5*/f32[3,7...) while((s32[]{:T(128)}, ...), condition=%wide.region_23.24_spmd.clone.clone, body=%wide.region_22.23_spmd.clone.clone.sunk | while | flops 352552384 | bytes 5641843 | solution.py:48
  904.0 3.2 bitcast_subtract_fusion
  (913 shorter events, 568.7 us)
Async XLA Ops:
  0.6 20.9 %collective-permute-start.2 = (f32[1,1,7,2,128,128]{5,4,3,2,0,1:T(8,128)}, f32[1,1,7,2,128,128]{5,4,3,2,0,1:T(8,128)S(1)}, u32[]{:S(2)}, u32[]{:S(2)}) collective-permute-start(f32[1,1,7,2,128,128]{5,4,3,2,0,1:T(8,128)} %bitcast.631), channel_id=1, source_target_pairs={{0,8},{8,16},{16,24},{24,0},{1,9},{9,17},{17,25},{25,1},{2,10},{10... | collective-permute-start | bytes 2752520 | tf_op jit(solution)/shard_map/ppermute | solution.py:15
  1.1 23.0 %collective-permute-start.3 = (f32[1,1,7,2,128,128]{5,4,3,2,0,1:T(8,128)}, f32[1,1,7,2,128,128]{5,4,3,2,0,1:T(8,128)}, u32[]{:S(2)}, u32[]{:S(2)}) collective-permute-start(f32[1,1,7,2,128,128]{5,4,3,2,0,1:T(8,128)} %bitcast.632), channel_id=1, source_target_pairs={{8,0},{16,8},{24,16},{0,24},{9,1},{17,9},{25,17},{1,25},{10,2},{18... | collective-permute-start | bytes 2752520 | tf_op jit(solution)/shard_map/ppermute | solution.py:18
  3.2 41.9 %collective-permute-start = (f32[1,1,7,2,128,128]{5,4,3,2,1,0:T(8,128)}, f32[1,1,7,2,128,128]{5,4,3,2,1,0:T(8,128)S(1)}, u32[]{:S(2)}, u32[]{:S(2)}) collective-permute-start(f32[1,1,7,2,128,128]{5,4,3,2,1,0:T(8,128)} %param.23), channel_id=1, source_target_pairs={{0,1},{1,2},{2,3},{3,4},{4,5},{5,6},{6,7},{7,0},{8,9},{9,10},{10,1... | collective-permute-start | bytes 2752520 | tf_op jit(solution)/shard_map/ppermute | solution.py:15
  5.4 41.8 %collective-permute-start.1 = (f32[1,1,7,2,128,128]{5,4,3,2,1,0:T(8,128)}, f32[1,1,7,2,128,128]{5,4,3,2,1,0:T(8,128)}, u32[]{:S(2)}, u32[]{:S(2)}) collective-permute-start(f32[1,1,7,2,128,128]{5,4,3,2,1,0:T(8,128)} %param.23), channel_id=1, source_target_pairs={{1,0},{2,1},{3,2},{4,3},{5,4},{6,5},{7,6},{0,7},{9,8},{10,9},{11,1... | collective-permute-start | bytes 2752520 | tf_op jit(solution)/shard_map/ppermute | solution.py:18
  14.9 32.4 %copy-start.2 = (f32[1,1,7,2,128,128]{5,4,3,2,1,0:T(8,128)S(1)}, f32[1,1,7,2,128,128]{5,4,3,2,1,0:T(8,128)}, u32[]{:S(2)}) copy-start(f32[1,1,7,2,128,128]{5,4,3,2,1,0:T(8,128)} %param.23) | copy-start | bytes 2752516
  123.4 43.4 %copy-start = (f32[1,1,7,2,128,128]{5,4,3,2,1,0:T(8,128)}, f32[1,1,7,2,128,128]{5,4,3,2,1,0:T(8,128)S(1)}, u32[]{:S(2)}) copy-start(f32[1,1,7,2,128,128]{5,4,3,2,1,0:T(8,128)S(1)} %fusion.221) | copy-start | bytes 2752516
  123.4 21.9 %collective-permute-start.6 = (f32[1,1,7,2,128,128]{5,4,3,2,1,0:T(8,128)S(1)}, f32[1,1,7,2,128,128]{5,4,3,2,1,0:T(8,128)S(1)}, u32[]{:S(2)}, u32[]{:S(2)}) collective-permute-start(f32[1,1,7,2,128,128]{5,4,3,2,1,0:T(8,128)S(1)} %fusion.221), channel_id=1, source_target_pairs={{0,8},{8,16},{16,24},{24,0},{1,9},{9,17},{17,25},{25,1},{2,10},{10... | collective-permute-start | bytes 2752520 | tf_op jit(solution)/shard_map/ppermute | solution.py:15
  123.5 21.9 %collective-permute-start.7 = (f32[1,1,7,2,128,128]{5,4,3,2,1,0:T(8,128)S(1)}, f32[1,1,7,2,128,128]{5,4,3,2,1,0:T(8,128)}, u32[]{:S(2)}, u32[]{:S(2)}) collective-permute-start(f32[1,1,7,2,128,128]{5,4,3,2,1,0:T(8,128)S(1)} %fusion.221), channel_id=1, source_target_pairs={{8,0},{16,8},{24,16},{0,24},{9,1},{17,9},{25,17},{1,25},{10,2},{18... | collective-permute-start | bytes 2752520 | tf_op jit(solution)/shard_map/ppermute | solution.py:18
  125.2 38.6 %collective-permute-start.4 = (f32[1,1,7,2,128,128]{5,4,3,2,1,0:T(8,128)S(1)}, f32[1,1,7,2,128,128]{5,4,3,2,1,0:T(8,128)S(1)}, u32[]{:S(2)}, u32[]{:S(2)}) collective-permute-start(f32[1,1,7,2,128,128]{5,4,3,2,1,0:T(8,128)S(1)} %fusion.221), channel_id=1, source_target_pairs={{0,1},{1,2},{2,3},{3,4},{4,5},{5,6},{6,7},{7,0},{8,9},{9,10},{10,1... | collective-permute-start | bytes 2752520 | tf_op jit(solution)/shard_map/ppermute | solution.py:15
  125.4 41.4 %collective-permute-start.5 = (f32[1,1,7,2,128,128]{5,4,3,2,1,0:T(8,128)S(1)}, f32[1,1,7,2,128,128]{5,4,3,2,1,0:T(8,128)}, u32[]{:S(2)}, u32[]{:S(2)}) collective-permute-start(f32[1,1,7,2,128,128]{5,4,3,2,1,0:T(8,128)S(1)} %fusion.221), channel_id=1, source_target_pairs={{1,0},{2,1},{3,2},{4,3},{5,4},{6,5},{7,6},{0,7},{9,8},{10,9},{11,1... | collective-permute-start | bytes 2752520 | tf_op jit(solution)/shard_map/ppermute | solution.py:18
  235.7 0.9 copy-start.3
  235.8 9.6 %copy-start.6 = (s32[7,3]{0,1:T(4,128)S(1)}, s32[7,3]{0,1:T(4,128)}, u32[]{:S(2)}) copy-start(s32[7,3]{0,1:T(4,128)} %param.25) | copy-start | bytes 256
  238.9 20.8 %collective-permute-start.10 = (f32[1,1,7,2,128,128]{5,4,3,2,1,0:T(8,128)S(1)}, f32[1,1,7,2,128,128]{5,4,3,2,1,0:T(8,128)S(1)}, u32[]{:S(2)}, u32[]{:S(2)}) collective-permute-start(f32[1,1,7,2,128,128]{5,4,3,2,1,0:T(8,128)S(1)} %fusion.219), channel_id=1, source_target_pairs={{0,8},{8,16},{16,24},{24,0},{1,9},{9,17},{17,25},{25,1},{2,10},{10... | collective-permute-start | bytes 2752520 | tf_op jit(solution)/shard_map/ppermute | solution.py:15
  238.9 21.7 %collective-permute-start.11 = (f32[1,1,7,2,128,128]{5,4,3,2,1,0:T(8,128)S(1)}, f32[1,1,7,2,128,128]{5,4,3,2,1,0:T(8,128)}, u32[]{:S(2)}, u32[]{:S(2)}) collective-permute-start(f32[1,1,7,2,128,128]{5,4,3,2,1,0:T(8,128)S(1)} %fusion.219), channel_id=1, source_target_pairs={{8,0},{16,8},{24,16},{0,24},{9,1},{17,9},{25,17},{1,25},{10,2},{18... | collective-permute-start | bytes 2752520 | tf_op jit(solution)/shard_map/ppermute | solution.py:18
  240.7 39.6 %collective-permute-start.8 = (f32[1,1,7,2,128,128]{5,4,3,2,1,0:T(8,128)S(1)}, f32[1,1,7,2,128,128]{5,4,3,2,1,0:T(8,128)S(1)}, u32[]{:S(2)}, u32[]{:S(2)}) collective-permute-start(f32[1,1,7,2,128,128]{5,4,3,2,1,0:T(8,128)S(1)} %fusion.219), channel_id=1, source_target_pairs={{0,1},{1,2},{2,3},{3,4},{4,5},{5,6},{6,7},{7,0},{8,9},{9,10},{10,1... | collective-permute-start | bytes 2752520 | tf_op jit(solution)/shard_map/ppermute | solution.py:15
  240.7 42.8 %collective-permute-start.9 = (f32[1,1,7,2,128,128]{5,4,3,2,1,0:T(8,128)S(1)}, f32[1,1,7,2,128,128]{5,4,3,2,1,0:T(8,128)}, u32[]{:S(2)}, u32[]{:S(2)}) collective-permute-start(f32[1,1,7,2,128,128]{5,4,3,2,1,0:T(8,128)S(1)} %fusion.219), channel_id=1, source_target_pairs={{1,0},{2,1},{3,2},{4,3},{5,4},{6,5},{7,6},{0,7},{9,8},{10,9},{11,1... | collective-permute-start | bytes 2752520 | tf_op jit(solution)/shard_map/ppermute | solution.py:18
  357.7 46.2 %copy-start.1 = (f32[1,1,7,2,128,128]{5,4,3,2,1,0:T(8,128)S(1)}, f32[1,1,7,2,128,128]{5,4,3,2,1,0:T(8,128)}, u32[]{:S(2)}) copy-start(f32[1,1,7,2,128,128]{5,4,3,2,1,0:T(8,128)} %param.24) | copy-start | bytes 2752516
  402.6 25.6 %copy-start.7 = (f32[2]{0:T(128)}, f32[2]{0:T(128)S(1)}, u32[]{:S(2)}) copy-start(f32[2]{0:T(128)S(1)} %maximum_multiply_fusion) | copy-start | bytes 28
  404.0 19.9 %collective-permute-start.14 = (f32[1,1,7,2,128,128]{5,4,3,2,1,0:T(8,128)S(1)}, f32[1,1,7,2,128,128]{5,4,3,2,1,0:T(8,128)S(1)}, u32[]{:S(2)}, u32[]{:S(2)}) collective-permute-start(f32[1,1,7,2,128,128]{5,4,3,2,1,0:T(8,128)S(1)} %broadcast_add_fusion), channel_id=1, source_target_pairs={{0,8},{8,16},{16,24},{24,0},{1,9},{9,17},{17,25},{25,1},{2,10},{10... | collective-permute-start | bytes 2752520 | tf_op jit(solution)/shard_map/ppermute | solution.py:15
  404.1 22.3 %collective-permute-start.15 = (f32[1,1,7,2,128,128]{5,4,3,2,1,0:T(8,128)S(1)}, f32[1,1,7,2,128,128]{5,4,3,2,1,0:T(8,128)S(1)}, u32[]{:S(2)}, u32[]{:S(2)}) collective-permute-start(f32[1,1,7,2,128,128]{5,4,3,2,1,0:T(8,128)S(1)} %broadcast_add_fusion), channel_id=1, source_target_pairs={{8,0},{16,8},{24,16},{0,24},{9,1},{17,9},{25,17},{1,25},{10,2},{18... | collective-permute-start | bytes 2752520 | tf_op jit(solution)/shard_map/ppermute | solution.py:18
  406.4 90.9 %collective-permute-start.12 = (f32[1,1,7,2,128,128]{5,4,3,2,1,0:T(8,128)S(1)}, f32[1,1,7,2,128,128]{5,4,3,2,1,0:T(8,128)}, u32[]{:S(2)}, u32[]{:S(2)}) collective-permute-start(f32[1,1,7,2,128,128]{5,4,3,2,1,0:T(8,128)S(1)} %broadcast_add_fusion), channel_id=1, source_target_pairs={{0,1},{1,2},{2,3},{3,4},{4,5},{5,6},{6,7},{7,0},{8,9},{9,10},{10,1... | collective-permute-start | bytes 2752520 | tf_op jit(solution)/shard_map/ppermute | solution.py:15
  408.8 88.6 %collective-permute-start.13 = (f32[1,1,7,2,128,128]{5,4,3,2,1,0:T(8,128)S(1)}, f32[1,1,7,2,128,128]{5,4,3,2,1,0:T(8,128)}, u32[]{:S(2)}, u32[]{:S(2)}) collective-permute-start(f32[1,1,7,2,128,128]{5,4,3,2,1,0:T(8,128)S(1)} %broadcast_add_fusion), channel_id=1, source_target_pairs={{1,0},{2,1},{3,2},{4,3},{5,4},{6,5},{7,6},{0,7},{9,8},{10,9},{11,1... | collective-permute-start | bytes 2752520 | tf_op jit(solution)/shard_map/ppermute | solution.py:18
  568.0 0.9 copy-start.4
  571.5 20.8 %collective-permute-start.18 = (f32[1,1,7,2,128,128]{5,4,3,2,1,0:T(8,128)S(1)}, f32[1,1,7,2,128,128]{5,4,3,2,1,0:T(8,128)S(1)}, u32[]{:S(2)}, u32[]{:S(2)}) collective-permute-start(f32[1,1,7,2,128,128]{5,4,3,2,1,0:T(8,128)S(1)} %bitcast_subtract_fusion.2), channel_id=1, source_target_pairs={{0,8},{8,16},{16,24},{24,0},{1,9},{9,17},{17,25},{25,1},{2,10},{10... | collective-permute-start | bytes 2752520 | tf_op jit(solution)/shard_map/ppermute | solution.py:15
  572.1 22.3 %collective-permute-start.19 = (f32[1,1,7,2,128,128]{5,4,3,2,1,0:T(8,128)S(1)}, f32[1,1,7,2,128,128]{5,4,3,2,1,0:T(8,128)S(1)}, u32[]{:S(2)}, u32[]{:S(2)}) collective-permute-start(f32[1,1,7,2,128,128]{5,4,3,2,1,0:T(8,128)S(1)} %bitcast_subtract_fusion.2), channel_id=1, source_target_pairs={{8,0},{16,8},{24,16},{0,24},{9,1},{17,9},{25,17},{1,25},{10,2},{18... | collective-permute-start | bytes 2752520 | tf_op jit(solution)/shard_map/ppermute | solution.py:18
  574.6 92.3 %collective-permute-start.16 = (f32[1,1,7,2,128,128]{5,4,3,2,1,0:T(8,128)S(1)}, f32[1,1,7,2,128,128]{5,4,3,2,1,0:T(8,128)}, u32[]{:S(2)}, u32[]{:S(2)}) collective-permute-start(f32[1,1,7,2,128,128]{5,4,3,2,1,0:T(8,128)S(1)} %bitcast_subtract_fusion.2), channel_id=1, source_target_pairs={{0,1},{1,2},{2,3},{3,4},{4,5},{5,6},{6,7},{7,0},{8,9},{9,10},{10,1... | collective-permute-start | bytes 2752520 | tf_op jit(solution)/shard_map/ppermute | solution.py:15
  575.7 91.2 %collective-permute-start.17 = (f32[1,1,7,2,128,128]{5,4,3,2,1,0:T(8,128)S(1)}, f32[1,1,7,2,128,128]{5,4,3,2,1,0:T(8,128)}, u32[]{:S(2)}, u32[]{:S(2)}) collective-permute-start(f32[1,1,7,2,128,128]{5,4,3,2,1,0:T(8,128)S(1)} %bitcast_subtract_fusion.2), channel_id=1, source_target_pairs={{1,0},{2,1},{3,2},{4,3},{5,4},{6,5},{7,6},{0,7},{9,8},{10,9},{11,1... | collective-permute-start | bytes 2752520 | tf_op jit(solution)/shard_map/ppermute | solution.py:18
  744.2 21.5 %collective-permute-start.22 = (f32[1,1,7,2,128,128]{5,4,3,2,1,0:T(8,128)}, f32[1,1,7,2,128,128]{5,4,3,2,1,0:T(8,128)S(1)}, u32[]{:S(2)}, u32[]{:S(2)}) collective-permute-start(f32[1,1,7,2,128,128]{5,4,3,2,1,0:T(8,128)} %bitcast_subtract_fusion.1), channel_id=1, source_target_pairs={{0,8},{8,16},{16,24},{24,0},{1,9},{9,17},{17,25},{25,1},{2,10},{10... | collective-permute-start | bytes 2752520 | tf_op jit(solution)/shard_map/ppermute | solution.py:15
  744.8 22.0 %collective-permute-start.23 = (f32[1,1,7,2,128,128]{5,4,3,2,1,0:T(8,128)}, f32[1,1,7,2,128,128]{5,4,3,2,1,0:T(8,128)S(1)}, u32[]{:S(2)}, u32[]{:S(2)}) collective-permute-start(f32[1,1,7,2,128,128]{5,4,3,2,1,0:T(8,128)} %bitcast_subtract_fusion.1), channel_id=1, source_target_pairs={{8,0},{16,8},{24,16},{0,24},{9,1},{17,9},{25,17},{1,25},{10,2},{18... | collective-permute-start | bytes 2752520 | tf_op jit(solution)/shard_map/ppermute | solution.py:18
  747.1 87.2 %collective-permute-start.20 = (f32[1,1,7,2,128,128]{5,4,3,2,1,0:T(8,128)}, f32[1,1,7,2,128,128]{5,4,3,2,1,0:T(8,128)}, u32[]{:S(2)}, u32[]{:S(2)}) collective-permute-start(f32[1,1,7,2,128,128]{5,4,3,2,1,0:T(8,128)} %bitcast_subtract_fusion.1), channel_id=1, source_target_pairs={{0,1},{1,2},{2,3},{3,4},{4,5},{5,6},{6,7},{7,0},{8,9},{9,10},{10,1... | collective-permute-start | bytes 2752520 | tf_op jit(solution)/shard_map/ppermute | solution.py:15
  747.2 87.1 %collective-permute-start.21 = (f32[1,1,7,2,128,128]{5,4,3,2,1,0:T(8,128)}, f32[1,1,7,2,128,128]{5,4,3,2,1,0:T(8,128)}, u32[]{:S(2)}, u32[]{:S(2)}) collective-permute-start(f32[1,1,7,2,128,128]{5,4,3,2,1,0:T(8,128)} %bitcast_subtract_fusion.1), channel_id=1, source_target_pairs={{1,0},{2,1},{3,2},{4,3},{5,4},{6,5},{7,6},{0,7},{9,8},{10,9},{11,1... | collective-permute-start | bytes 2752520 | tf_op jit(solution)/shard_map/ppermute | solution.py:18
  834.3 4.0 copy-start.5
where the time goes:
time: 915 us; the launch traced here: 907 us
  local copies, waits for them, and re-layouts  402 us (44%)
  waiting for transfers between devices  143 us (16%)
  loops' own time  122 us (13%)
  matrix products  90.8 us (10%)
  other arithmetic  64.9 us (7%)
  starting transfers between devices  41.7 us (5%)
  blocking collectives  39.5 us (4%)
    gather x63, local copies, waits for them, and re-layouts, one_target(): right_part = right_rim[row_pick[:, None], partners_row[:, None], layer_pick]  153 us
    gather x63, local copies, waits for them, and re-layouts, one_target(): left_rim[col_pick[partners_row], left_slots]  151 us
    ppermute x12, waiting for transfers between devices, with_halo(): lax.ppermute(lax.slice_in_dim(block, block.shape[dim] - width, None, axis...  125 us
    another operation x9, loops' own time, sparse_product(): return lax.map(one_target, jnp.arange(count_offsets, dtype=jnp.int32))  122 us
    dot_general x63, matrix products, one_target(): jnp.einsum('tsab,tsbc->sac', left_part, right_part, precision=FULL_PRECIS...  90.8 us
    gather x63, local copies, waits for them, and re-layouts, one_target(): col_pick[partners_row]  40.5 us
    psum x1, blocking collectives, local(): lax.psum((jnp.sum(hamiltonian * new_density), jnp.sum(new_density * ident...  39.5 us
    dynamic_slice x63, local copies, waits for them, and re-layouts, sparse_product(): return lax.map(one_target, jnp.arange(count_offsets, dtype=jnp.int32))  37.9 us
  transfers between devices with their start and end apart: 24, of which 17 were waited for; matrix products, arithmetic and copies ran while one was open for 21% of the time, Pallas kernels for 0%

commit v1 on v0

--- a/solution.py
+++ b/solution.py
@@ -1,7 +1,448 @@
+import functools
+
 import jax
 import jax.numpy as jnp
 from jax import lax
+from jax.experimental import pallas as pl
+from jax.experimental.pallas import tpu as pltpu
 from jax.sharding import PartitionSpec as P
+
+F32 = jnp.float32
+BF16 = jnp.bfloat16
+EXTRA = 8
+
+
+def iotas(size):
+    shape = (size, size)
+    return lax.broadcasted_iota(jnp.int32, shape, 0), lax.broadcasted_iota(jnp.int32, shape, 1)
+
+
+def store_split(dst, index, value):
+    size = value.shape[-1]
+    high = value.astype(BF16)
+    dst[index + (slice(None), slice(0, size))] = high
+    dst[index + (slice(None), slice(size, 2 * size))] = (value - high.astype(F32)).astype(BF16)
+
+
+def quadrants(q):
+    size = q.shape[-1] // 2
+    return (q[:size, :size] + q[size:, size:]) + (q[:size, size:] + q[size:, :size])
+
+
+def pack_pair(first, second):
+    size = first.shape[-1]
+    row, col = iotas(size)
+    body = jnp.where(row <= col, first, second)
+    diagonal = jnp.sum(jnp.where(row == col, second, 0.0), axis=0, keepdims=True)
+    return jnp.concatenate([body, jnp.broadcast_to(diagonal, (EXTRA, size))], axis=0)
+
+
+def unpack_pair(packed):
+    size = packed.shape[-1]
+    row, col = iotas(size)
+    body = packed[:size]
+    turned = body.T
+    second_diagonal = packed[size : size + 1]
+    first = jnp.where(row <= col, body, turned)
+    second = jnp.where(row > col, body, jnp.where(row == col, second_diagonal, turned))
+    return first, second
+
+
+def slot_offsets(off, t, layers):
+    return off[t, 0], off[t, 1], lax.rem(off[t, 2] + layers, layers)
+
+
+def zero_slot(off, slots):
+    z = jnp.int32(0)
+    for t in range(slots):
+        hit = (off[t, 0] == 0) & (off[t, 1] == 0) & (off[t, 2] == 0)
+        z = jnp.where(hit, jnp.int32(t), z)
+    return z
+
+
+def sign_of(branch, k):
+    return (2 * branch[k] - 1).astype(F32)
+
+
+def vertex_sums(off, left, right, acc, keep):
+    slots, layers = left.shape[0], left.shape[1]
+    acc[...] = jnp.zeros_like(acc)
+    for t in range(slots):
+        r, _, l = slot_offsets(off, t, layers)
+
+        def add(t=t, r=r, l=l):
+            for s in range(layers):
+                q = lax.dot_general(
+                    left[t, s], right[t, s], (((0,), (0,)), ((), ())), preferred_element_type=F32
+                )
+                acc[r + 1, lax.rem(s + l, layers)] += quadrants(q)
+
+        if keep is None:
+            add()
+        else:
+            pl.when(keep(r))(add)
+
+
+def symmetric(value):
+    return value + value.T
+
+
+def edge_product(lefts, rights):
+    size = lefts[0].shape[0]
+    high = [x[:, :size] for x in lefts]
+    low = [x[:, size:] for x in lefts]
+    lhs = jnp.concatenate([jnp.concatenate(high, 1), jnp.concatenate(low, 1)], 0)
+    rhs = jnp.concatenate(rights, 0)
+    return quadrants(jnp.dot(lhs, rhs, preferred_element_type=F32))
+
+
+def fill_neighbours(dst, own, low, high, which):
+    for k in range(dst.shape[1] // 2):
+        for slot, message in ((0, low), (2, high)):
+            first, second = unpack_pair(message[which, k])
+            store_split(dst, (slot, 2 * k), first)
+            store_split(dst, (slot, 2 * k + 1), second)
+    for s in range(dst.shape[1]):
+        store_split(dst, (1, s), own[s])
+
+
+def add_sums(value, low, high, which):
+    out = list(value)
+    for k in range(len(out) // 2):
+        for message in (low, high):
+            first, second = unpack_pair(message[which, k])
+            out[2 * k] = out[2 * k] + first
+            out[2 * k + 1] = out[2 * k + 1] + second
+    return out
+
+
+def put_pairs(ref, which, blocks):
+    for k in range(len(blocks) // 2):
+        ref[which, k] = pack_pair(blocks[2 * k], blocks[2 * k + 1])
+
+
+def split_all(src, dst):
+    for t in range(src.shape[0]):
+        for s in range(src.shape[1]):
+            store_split(dst, (t, s), src[t, s])
+
+
+def send_sums(acc, which, up, down, sym):
+    layers = acc.shape[1]
+    for r, ref in ((2, up), (0, down)):
+        blocks = [acc[r, s] for s in range(layers)]
+        put_pairs(ref, which, [symmetric(b) for b in blocks] if sym else blocks)
+
+
+def start_kernel(off, x, h, up, down, side, x_local, xs, acc):
+    slots, layers = x.shape[0], x.shape[1]
+    z = zero_slot(off, slots)
+    split_all(x, xs)
+    vertex_sums(off, xs, xs, acc, None)
+    diag = [x[z, s] for s in range(layers)]
+    diag_h = [h[z, s] for s in range(layers)]
+    for ref in (up, down, side):
+        put_pairs(ref, 0, diag)
+        put_pairs(ref, 1, diag_h)
+    send_sums(acc, 2, up, down, False)
+    for s in range(layers):
+        x_local[s] = acc[1, s]
+
+
+def square_step(off, s_k, x, x_local, row_low, row_high, col_low, col_high, new, xs, rows, cols, sums_at):
+    slots, layers = x.shape[0], x.shape[1]
+    z = zero_slot(off, slots)
+    split_all(x, xs)
+    own = [x[z, s] for s in range(layers)]
+    fill_neighbours(rows, own, row_low, row_high, 0)
+    fill_neighbours(cols, own, col_low, col_high, 0)
+    square = add_sums([x_local[s] for s in range(layers)], row_low, row_high, sums_at)
+    for s in range(layers):
+        new[z, s] = own[s] + s_k * (own[s] - square[s])
+    for i in range(slots - 1):
+        t = i + (i >= z).astype(jnp.int32)
+        r, c, l = slot_offsets(off, t, layers)
+        for s in range(layers):
+            e = xs[t, s]
+            product = edge_product([cols[1 - c, s], e], [e, rows[1 + r, lax.rem(s + l, layers)]])
+            e32 = x[t, s]
+            new[t, s] = e32 + s_k * (e32 - product)
+    return z
+
+
+def square_kernel(k, sums_at, off, branch, x, x_local, row_low, row_high, col_low, col_high,
+                  new, up, down, side, new_local, xs, ns, rows, cols, acc):
+    layers = x.shape[1]
+    z = square_step(off, sign_of(branch, k), x, x_local, row_low, row_high, col_low, col_high,
+                    new, xs, rows, cols, sums_at)
+    diag = [new[z, s] for s in range(layers)]
+    for ref in (up, down, side):
+        put_pairs(ref, 0, diag)
+    split_all(new, ns)
+    vertex_sums(off, ns, ns, acc, None)
+    send_sums(acc, 1, up, down, False)
+    for s in range(layers):
+        new_local[s] = acc[1, s]
+
+
+def last_square_kernel(k, sums_at, off, branch, x, x_local, row_low, row_high, col_low, col_high, h,
+                       new, sums, xs, rows, cols):
+    slots, layers, size = x.shape[0], x.shape[1], x.shape[2]
+    z = square_step(off, sign_of(branch, k), x, x_local, row_low, row_high, col_low, col_high,
+                    new, xs, rows, cols, sums_at)
+    energy = jnp.zeros((size, size), F32)
+    for t in range(slots):
+        for s in range(layers):
+            energy = energy + h[t, s] * new[t, s]
+    row, col = iotas(size)
+    trace = jnp.zeros((size, size), F32)
+    for s in range(layers):
+        trace = trace + jnp.where(row == col, new[z, s], 0.0)
+    sums[0:1, :] = jnp.broadcast_to(jnp.sum(energy, keepdims=True), (1, size))
+    sums[1:2, :] = jnp.broadcast_to(jnp.sum(trace, keepdims=True), (1, size))
+    sums[2:, :] = jnp.zeros_like(sums[2:, :])
+
+
+def turn_square_kernel(k, off, branch, x, x_local, row_low, row_high, col_low, col_high, h,
+                       new, up, down, side, new_local, h_local, cross_local,
+                       xs, hs, news, rows, cols, acc):
+    slots, layers = x.shape[0], x.shape[1]
+    z = square_step(off, sign_of(branch, k), x, x_local, row_low, row_high, col_low, col_high,
+                    new, xs, rows, cols, 1)
+    diag = [new[z, s] for s in range(layers)]
+    for ref in (up, down, side):
+        put_pairs(ref, 0, diag)
+    split_all(new, news)
+    split_all(h, hs)
+    vertex_sums(off, news, news, acc, None)
+    send_sums(acc, 1, up, down, False)
+    for s in range(layers):
+        new_local[s] = acc[1, s]
+    vertex_sums(off, hs, news, acc, None)
+    send_sums(acc, 2, up, down, True)
+    for s in range(layers):
+        h_local[s] = symmetric(acc[1, s])
+    vertex_sums(off, news, xs, acc, None)
+    send_sums(acc, 3, up, down, True)
+    for s in range(layers):
+        cross_local[s] = symmetric(acc[1, s])
+
+
+def gradient_edges(off, s_k, g, new, gs, xs, g_rows, g_cols, x_rows, x_cols, z):
+    slots, layers = g.shape[0], g.shape[1]
+    for i in range(slots - 1):
+        t = i + (i >= z).astype(jnp.int32)
+        r, c, l = slot_offsets(off, t, layers)
+        for s in range(layers):
+            e, f = gs[t, s], xs[t, s]
+            b = lax.rem(s + l, layers)
+            product = edge_product(
+                [g_cols[1 - c, s], x_cols[1 - c, s], e, f], [f, e, x_rows[1 + r, b], g_rows[1 + r, b]]
+            )
+            new[t, s] = (1.0 + s_k) * g[t, s] - s_k * product
+
+
+def first_gradient_kernel(k, off, branch, h, x, x_before, h_local, h_row_low, h_row_high, h_col_low, h_col_high,
+                          row_low, row_high, col_low, col_high,
+                          new, up, down, side, new_local,
+                          gs, xs, ns, bs, g_rows, g_cols, x_rows, x_cols, acc):
+    layers = x.shape[1]
+    s_k = sign_of(branch, k)
+    z = zero_slot(off, x.shape[0])
+    split_all(h, gs)
+    split_all(x, xs)
+    own_h = [h[z, s] for s in range(layers)]
+    own_x = [x[z, s] for s in range(layers)]
+    fill_neighbours(g_rows, own_h, h_row_low, h_row_high, 1)
+    fill_neighbours(g_cols, own_h, h_col_low, h_col_high, 1)
+    fill_neighbours(x_rows, own_x, row_low, row_high, 0)
+    fill_neighbours(x_cols, own_x, col_low, col_high, 0)
+    cross = add_sums([h_local[s] for s in range(layers)], row_low, row_high, 2)
+    for s in range(layers):
+        new[z, s] = (1.0 + s_k) * own_h[s] - s_k * cross[s]
+    gradient_edges(off, s_k, h, new, gs, xs, g_rows, g_cols, x_rows, x_cols, z)
+    diag = [new[z, s] for s in range(layers)]
+    for ref in (up, down, side):
+        put_pairs(ref, 0, diag)
+    split_all(new, ns)
+    split_all(x_before, bs)
+    vertex_sums(off, ns, bs, acc, None)
+    send_sums(acc, 1, up, down, True)
+    for s in range(layers):
+        new_local[s] = symmetric(acc[1, s])
+
+
+def next_gradient_kernel(k, order, off, branch, sums, gh, x_after, x, x_before, gh_local, cross_local,
+                         g_row_low, g_row_high, g_col_low, g_col_high,
+                         after_row_low, after_row_high, after_col_low, after_col_high,
+                         row_low, row_high, col_low, col_high,
+                         new, up, down, side, new_local,
+                         g, gs, xs, ns, bs, g_rows, g_cols, x_rows, x_cols, acc):
+    slots, layers, size = x.shape[0], x.shape[1], x.shape[2]
+    s_k = sign_of(branch, k)
+    s_after = sign_of(branch, k + 1)
+    excess = sums[1:2, :] * (1.0 / order) - 0.5
+    z = zero_slot(off, slots)
+    row, col = iotas(size)
+    eye = jnp.where(row == col, excess * (1.0 + s_after), 0.0)
+    scale = excess * (-2.0 * s_after)
+    for t in range(slots):
+        for s in range(layers):
+            g[t, s] = gh[t, s] + scale * x_after[t, s]
+    for s in range(layers):
+        g[z, s] = g[z, s] + eye
+    split_all(g, gs)
+    split_all(x, xs)
+    own_g = [g[z, s] for s in range(layers)]
+    own_x = [x[z, s] for s in range(layers)]
+    for dst, pairs in (
+        (g_rows, ((0, g_row_low, after_row_low), (2, g_row_high, after_row_high))),
+        (g_cols, ((0, g_col_low, after_col_low), (2, g_col_high, after_col_high))),
+    ):
+        for slot, message, after in pairs:
+            for j in range(layers // 2):
+                blocks = unpack_pair(message[0, j])
+                befores = unpack_pair(after[0, j])
+                for p in range(2):
+                    store_split(dst, (slot, 2 * j + p), blocks[p] + scale * befores[p] + eye)
+        for s in range(layers):
+            store_split(dst, (1, s), own_g[s])
+    fill_neighbours(x_rows, own_x, row_low, row_high, 0)
+    fill_neighbours(x_cols, own_x, col_low, col_high, 0)
+    own_sums = add_sums([gh_local[s] for s in range(layers)], g_row_low, g_row_high, 1)
+    cross_sums = add_sums([cross_local[s] for s in range(layers)], after_row_low, after_row_high, 3)
+    twice = 2.0 * (1.0 + s_after) * excess
+    for s in range(layers):
+        cross = own_sums[s] + scale * cross_sums[s] + twice * own_x[s]
+        new[z, s] = (1.0 + s_k) * own_g[s] - s_k * cross
+    gradient_edges(off, s_k, g, new, gs, xs, g_rows, g_cols, x_rows, x_cols, z)
+    diag = [new[z, s] for s in range(layers)]
+    for ref in (up, down, side):
+        put_pairs(ref, 0, diag)
+    split_all(new, ns)
+    split_all(x_before, bs)
+    vertex_sums(off, ns, bs, acc, None)
+    send_sums(acc, 1, up, down, True)
+    for s in range(layers):
+        new_local[s] = symmetric(acc[1, s])
+
+
+def last_gradient_kernel(k, off, branch, g, x, g_local, g_row_low, g_row_high, g_col_low, g_col_high,
+                         row_low, row_high, col_low, col_high,
+                         new, gs, xs, g_rows, g_cols, x_rows, x_cols):
+    layers = x.shape[1]
+    s_k = sign_of(branch, k)
+    z = zero_slot(off, x.shape[0])
+    split_all(g, gs)
+    split_all(x, xs)
+    own_g = [g[z, s] for s in range(layers)]
+    own_x = [x[z, s] for s in range(layers)]
+    fill_neighbours(g_rows, own_g, g_row_low, g_row_high, 0)
+    fill_neighbours(g_cols, own_g, g_col_low, g_col_high, 0)
+    fill_neighbours(x_rows, own_x, row_low, row_high, 0)
+    fill_neighbours(x_cols, own_x, col_low, col_high, 0)
+    cross = add_sums([g_local[s] for s in range(layers)], g_row_low, g_row_high, 1)
+    for s in range(layers):
+        new[z, s] = (1.0 + s_k) * own_g[s] - s_k * cross[s]
+    gradient_edges(off, s_k, g, new, gs, xs, g_rows, g_cols, x_rows, x_cols, z)
+
+
+def call(kernel, smem, vmem, outs, scratch):
+    return pl.pallas_call(
+        kernel,
+        out_shape=[jax.ShapeDtypeStruct(shape, F32) for shape in outs],
+        in_specs=[pl.BlockSpec(memory_space=pltpu.SMEM)] * len(smem)
+        + [pl.BlockSpec(memory_space=pltpu.VMEM)] * len(vmem),
+        out_specs=[pl.BlockSpec(memory_space=pltpu.VMEM)] * len(outs),
+        scratch_shapes=scratch,
+        compiler_params=pltpu.CompilerParams(vmem_limit_bytes=40 * 1024 * 1024),
+    )(*smem, *vmem)
+
+
+def ring(axis):
+    count = lax.axis_size(axis)
+    forward = [(i, (i + 1) % count) for i in range(count)]
+    return forward, [(b, a) for a, b in forward]
+
+
+def exchange(up, down, side):
+    row_forward, row_backward = ring("row")
+    col_forward, col_backward = ring("col")
+    return (
+        lax.ppermute(up, "row", row_forward),
+        lax.ppermute(down, "row", row_backward),
+        lax.ppermute(side, "col", col_forward),
+        lax.ppermute(side, "col", col_backward),
+    )
+
+
+def total_over(value, axis):
+    count = lax.axis_size(axis)
+    if count & (count - 1):
+        return lax.psum(value, axis)
+    step = 1
+    while step < count:
+        value = value + lax.ppermute(value, axis, [(i, i ^ step) for i in range(count)])
+        step *= 2
+    return value
+
+
+def sparse_path(density, hamiltonian, offsets, branch):
+    slots, layers, size = density.shape[2:5]
+    full = (slots, layers, size, size)
+    x0 = density.reshape(full)
+    h = hamiltonian.reshape(full)
+    order = size * layers * lax.axis_size("row") * lax.axis_size("col")
+    pairs = layers // 2
+
+    def message(n):
+        return (n, pairs, size + EXTRA, size)
+
+    local = (layers, size, size)
+    split = pltpu.VMEM((slots, layers, size, 2 * size), BF16)
+    three = pltpu.VMEM((3, layers, size, 2 * size), BF16)
+    acc = pltpu.VMEM((3, layers, size, size), F32)
+    smem = (offsets, branch)
+    up, down, side, local0 = call(
+        start_kernel, (offsets,), (x0, h), [message(3), message(3), message(2), local], [split, acc]
+    )
+    near0 = exchange(up, down, side)
+    x1, up, down, side, local1 = call(
+        functools.partial(square_kernel, 0, 2), smem, (x0, local0, *near0),
+        [full, message(2), message(2), message(1), local], [split, split, three, three, acc],
+    )
+    near1 = exchange(up, down, side)
+    x2, up, down, side, local2, h_local, cross_local = call(
+        functools.partial(turn_square_kernel, 1), smem, (x1, local1, *near1, h),
+        [full, message(4), message(4), message(1), local, local, local],
+        [split, split, split, three, three, acc],
+    )
+    near2 = exchange(up, down, side)
+    gh, up, down, side, gh_local = call(
+        functools.partial(first_gradient_kernel, 2), smem, (h, x2, x1, h_local, *near0, *near2),
+        [full, message(2), message(2), message(1), local],
+        [split, split, split, split, three, three, three, three, acc],
+    )
+    near_gh = exchange(up, down, side)
+    x3, sums = call(
+        functools.partial(last_square_kernel, 2, 1), smem, (x2, local2, *near2, h),
+        [full, (8, size)], [split, three, three],
+    )
+    sums = total_over(total_over(sums, "row"), "col")
+    g1, up, down, side, g1_local = call(
+        functools.partial(next_gradient_kernel, 1, float(order)), smem,
+        (sums, gh, x2, x1, x0, gh_local, cross_local, *near_gh, *near2, *near1),
+        [full, message(2), message(2), message(1), local],
+        [pltpu.VMEM(full, F32), split, split, split, split, three, three, three, three, acc],
+    )
+    near_g1 = exchange(up, down, side)
+    (g0,) = call(
+        functools.partial(last_gradient_kernel, 0), smem, (g1, x0, g1_local, *near_g1, *near0),
+        [full], [split, split, three, three, three, three],
+    )
+    totals = sums[:2, 0] / order
+    return x3.reshape(density.shape), g0.reshape(density.shape), totals
+
 
 FULL_PRECISION = lax.Precision.HIGHEST
 
@@ -60,7 +501,7 @@
     return (cols_rim, rows_rim)
 
 
-def local(density, hamiltonian, offsets, branch):
+def general_path(density, hamiltonian, offsets, branch):
     row_count = lax.axis_size("row")
     col_count = lax.axis_size("col")
     step_count = branch.shape[0]
@@ -111,6 +552,16 @@
     return (new_density, outer_grad, totals)
 
 
+def local(density, hamiltonian, offsets, branch):
+    moduli = jnp.array([lax.axis_size("row"), lax.axis_size("col"), density.shape[3]], jnp.int32)
+    nonzero = jnp.any(offsets != 0, axis=1)
+    summed = offsets[:, None, :] + offsets[None, :, :]
+    differ = summed[None, :, :, :] - offsets[:, None, None, :]
+    matches = jnp.all(differ % moduli == 0, axis=-1)
+    closed = matches & nonzero[:, None, None] & nonzero[None, :, None] & nonzero[None, None, :]
+    return lax.cond(jnp.any(closed), general_path, sparse_path, density, hamiltonian, offsets, branch)
+
+
 def solution(mesh):
     return jax.shard_map(
         local,

time: 915 us -> 91.2 us (0.10)
  local copies, waits for them, and re-layouts: 402 us -> 1.63 us
  loops' own time: 122 us -> 0.18 us
  waiting for transfers between devices: 143 us -> 27.3 us
  matrix products: 90.8 us -> 0 us
  other arithmetic: 64.9 us -> 4.51 us
  blocking collectives: 39.5 us -> 0 us
  Pallas kernels: 0 us -> 21.6 us
    gather x189 -> x0, local copies, waits for them, and re-layouts: 344 us -> none  [the longest x63 153 us: one_target(): right_part = right_rim[row_pick[:, None], partners_row[:, None], layer_pick]]
    another operation x9 -> x1, loops' own time: 122 us -> 0.18 us  [local(): lax.cond(jnp.any(closed), general_path, sparse_path, density, hamiltonian...]
    ppermute x24 -> x25, waiting for transfers between devices: 143 us -> 27.3 us  [the longest x5 15.9 us: total_over(): lax.ppermute(value, axis, [(i, i ^ step) for i in range(count)])]
    dot_general x63 -> x0, matrix products: 90.8 us -> none  [one_target(): jnp.einsum('tsab,tsbc->sac', left_part, right_part, precision=FULL_PRECIS...]
    psum x1 -> x0, blocking collectives: 39.5 us -> none  [local(): lax.psum((jnp.sum(hamiltonian * new_density), jnp.sum(new_density * ident...]
    dynamic_slice x63 -> x0, local copies, waits for them, and re-layouts: 37.9 us -> none  [sparse_product(): return lax.map(one_target, jnp.arange(count_offsets, dtype=jnp.int32))]
    squeeze x12 -> x0, other arithmetic: 36.5 us -> none  [the longest x2 7.4 us: outer_rims(): cols_rim = with_halo(field, (('col', 1),), 1)[0]]
    pallas_call x0 -> x7, Pallas kernels: none -> 21.6 us  [call(): pl.pallas_call(kernel, out_shape=[jax.ShapeDtypeStruct(shape, F32) for sh...]
  transfers between devices with their start and end apart: 24 -> 25, of which waited for: 17 -> 10; matrix products, arithmetic and copies ran while one was open for 21% -> 1% of each run, Pallas kernels for 0% -> 3%
where the time goes in v1:
time: 91.2 us; the launch traced here: 91 us
  starting transfers between devices  34.4 us (38%)
  waiting for transfers between devices  27.3 us (30%)
  Pallas kernels  21.6 us (24%)
  other arithmetic  4.51 us (5%)
  local copies, waits for them, and re-layouts  1.63 us (2%)
  between operations  1.29 us (1%)
    pallas_call x7, Pallas kernels, call(): pl.pallas_call(kernel, out_shape=[jax.ShapeDtypeStruct(shape, F32) for sh...  21.6 us
    ppermute x5, starting transfers between devices, exchange(): lax.ppermute(side, 'col', col_backward)  20.4 us
    ppermute x5, waiting for transfers between devices, total_over(): lax.ppermute(value, axis, [(i, i ^ step) for i in range(count)])  15.9 us
    ppermute x5, waiting for transfers between devices, exchange(): lax.ppermute(side, 'col', col_forward)  10.1 us
    ppermute x5, starting transfers between devices, exchange(): lax.ppermute(down, 'row', row_backward)  8.9 us
    ppermute x5, starting transfers between devices, exchange(): lax.ppermute(side, 'col', col_forward)  3.75 us
  transfers between devices with their start and end apart: 25, of which 10 were waited for; matrix products, arithmetic and copies ran while one was open for 1% of the time, Pallas kernels for 3%

profile of v1, /device:TPU:0, one launch (start us, length us, event | category | flops | bytes accessed | tf_op | source)
XLA Modules:
  0.0 91.0 jit_solution(4810176476969210)
XLA Ops:
  2.2 1.6 %fusion.233 = pred[7,7,7]{2,1,0:T(8,128)(4,1)S(1)} fusion(s32[3]{0:T(128)} %constant.310.clone, s32[7,3]{1,0:T(8,128)S(1)} %copy.102, s32[7,7,3]{1,0,2:T(8,128)S(1)} %broadcast_add_fusion.2), kind=kLoop, calls=%fused_computation.408 | loop fusion | flops 8918 | bytes 1027 | tf_op jit(solution)/shard_map/reduce_and | solution.py:560
  5.9 85.0 %conditional.1 = (f32[1,1,7,2,128,128]{5,4,3,2,1,0:T(8,128)}, f32[1,1,7,2,128,128]{5,4,3,2,1,0:T(8,128)}, f32[2]{0:T(128)}) conditional(s32[]{:T(128)} %convert_element_type.122, (f32[1,1,7,2,128,128]{5,4,3,2,1,0:T(8,128)}, f32[1,1,7,2,128,128]{5,4,3,2,1,0:T(8,128)}, s32[7,3]{0,1:T(4,128)}, s32[3]{0:T(128)}) %tuple.81, (s32[3]{0:T(128)}, ...), branch_computations={%region_3.5_spmd, %region_4.32_spmd} | conditional | flops 3196069888 | bytes 259712128 | solution.py:562
  6.0 0.8 copy.103.off
  6.8 2.3 %branch_0_fun.7 = (f32[3,1,136,128]{3,2,1,0:T(8,128)S(1)}, f32[3,1,136,128]{3,2,1,0:T(8,128)S(1)}, f32[2,1,136,128]{3,2,1,0:T(8,128)S(1)}, f32[2,128,128]{2,1,0:T(8,128)S(1)}) custom-call(s32[7,3]{1,0:T(8,128)S(1)} %copy.103.off, f32[7,2,128,128]{3,2,1,0:T(8,128)} %bitcast.639, f32[7,2,128,128]{3,2,1,0:T(8,128)} %bitcast.635), custom_call_target="tpu_custom_call" | custom-call | tf_op jit(solution)/shard_map/cond/branch_0_fun/pallas_call | solution.py:351
  9.6 2.0 %collective-permute-start.1 = (f32[3,1,136,128]{3,2,1,0:T(8,128)S(1)}, f32[3,1,136,128]{3,2,1,0:T(8,128)S(1)}, u32[]{:S(2)}, u32[]{:S(2)}) collective-permute-start(f32[3,1,136,128]{3,2,1,0:T(8,128)S(1)} %get-tuple-element.637), channel_id=1, source_target_pairs={{8,0},{16,8},{24,16},{0,24},{9,1},{17,9},{25,17},{1,25},{10,2},{18... | collective-permute-start | bytes 626696 | tf_op jit(solution)/shard_map/cond/branch_0_fun/ppermute | solution.py:373
  11.6 2.2 %collective-permute-start.2 = (f32[2,1,136,128]{3,2,1,0:T(8,128)S(1)}, f32[2,1,136,128]{3,2,1,0:T(8,128)S(1)}, u32[]{:S(2)}, u32[]{:S(2)}) collective-permute-start(f32[2,1,136,128]{3,2,1,0:T(8,128)S(1)} %get-tuple-element.638), channel_id=1, source_target_pairs={{0,1},{1,2},{2,3},{3,4},{4,5},{5,6},{6,7},{7,0},{8,9},{9,10},{10,1... | collective-permute-start | bytes 417800 | tf_op jit(solution)/shard_map/cond/branch_0_fun/ppermute | solution.py:374
  13.8 3.0 %collective-permute-start.3 = (f32[2,1,136,128]{3,2,1,0:T(8,128)S(1)}, f32[2,1,136,128]{3,2,1,0:T(8,128)S(1)}, u32[]{:S(2)}, u32[]{:S(2)}) collective-permute-start(f32[2,1,136,128]{3,2,1,0:T(8,128)S(1)} %get-tuple-element.638), channel_id=1, source_target_pairs={{1,0},{2,1},{3,2},{4,3},{5,4},{6,5},{7,6},{0,7},{9,8},{10,9},{11,1... | collective-permute-start | bytes 417800 | tf_op jit(solution)/shard_map/cond/branch_0_fun/ppermute | solution.py:375
  16.8 3.8 %collective-permute-done.2.col_low.h_col_low = f32[2,1,136,128]{3,2,1,0:T(8,128)S(1)} collective-permute-done((f32[2,1,136,128]{3,2,1,0:T(8,128)S(1)}, f32[2,1,136,128]{3,2,1,0:T(8,128)S(1)}, u32[]{:S(2)}, u32[]{:S(2)}) %collective-permute-start.2) | collective-permute-done | bytes 139296 | tf_op jit(solution)/shard_map/cond/branch_0_fun/ppermute | solution.py:374
  20.7 1.3 %collective-permute-done.3.col_high.h_col_high = f32[2,1,136,128]{3,2,1,0:T(8,128)S(1)} collective-permute-done((f32[2,1,136,128]{3,2,1,0:T(8,128)S(1)}, f32[2,1,136,128]{3,2,1,0:T(8,128)S(1)}, u32[]{:S(2)}, u32[]{:S(2)}) %collective-permute-start.3) | collective-permute-done | bytes 139296 | tf_op jit(solution)/shard_map/cond/branch_0_fun/ppermute | solution.py:375
  22.0 3.0 %branch_0_fun.8 = (f32[7,2,128,128]{3,2,1,0:T(8,128)S(1)}, f32[2,1,136,128]{3,2,1,0:T(8,128)S(1)}, f32[2,1,136,128]{3,2,1,0:T(8,128)S(1)}, f32[1,1,136,128]{3,2,1,0:T(8,128)S(1)}, f32[2,128,128]{2,1,0:T(8,128)S(1)}) custom-call(s32[7,3]{1,0:T(8,128)S(1)} %copy.103.off, s32[3]{0:T(128)} %get-tuple-element.632.branch, f32[7,2,128,128]{3,2,1,0:T(8,128)} %bitcast.640, ...), custom_call_target="tpu_custom_call" | custom-call | tf_op jit(solution)/shard_map/cond/branch_0_fun/pallas_call | solution.py:351
  25.1 1.7 %collective-permute-start.5 = (f32[2,1,136,128]{3,2,1,0:T(8,128)S(1)}, f32[2,1,136,128]{3,2,1,0:T(8,128)S(1)}, u32[]{:S(2)}, u32[]{:S(2)}) collective-permute-start(f32[2,1,136,128]{3,2,1,0:T(8,128)S(1)} %get-tuple-element.642), channel_id=1, source_target_pairs={{8,0},{16,8},{24,16},{0,24},{9,1},{17,9},{25,17},{1,25},{10,2},{18... | collective-permute-start | bytes 417800 | tf_op jit(solution)/shard_map/cond/branch_0_fun/ppermute | solution.py:373
  27.1 4.4 %collective-permute-start.7 = (f32[1,1,136,128]{3,2,1,0:T(8,128)S(1)}, f32[1,1,136,128]{3,2,1,0:T(8,128)S(1)}, u32[]{:S(2)}, u32[]{:S(2)}) collective-permute-start(f32[1,1,136,128]{3,2,1,0:T(8,128)S(1)} %get-tuple-element.643), channel_id=1, source_target_pairs={{1,0},{2,1},{3,2},{4,3},{5,4},{6,5},{7,6},{0,7},{9,8},{10,9},{11,1... | collective-permute-start | bytes 208904 | tf_op jit(solution)/shard_map/cond/branch_0_fun/ppermute | solution.py:375
  31.6 2.3 %collective-permute-done.6.col_low = f32[1,1,136,128]{3,2,1,0:T(8,128)S(1)} collective-permute-done((f32[1,1,136,128]{3,2,1,0:T(8,128)S(1)}, f32[1,1,136,128]{3,2,1,0:T(8,128)S(1)}, u32[]{:S(2)}, u32[]{:S(2)}) %collective-permute-start.6) | collective-permute-done | bytes 69664 | tf_op jit(solution)/shard_map/cond/branch_0_fun/ppermute | solution.py:374
  33.9 3.8 %branch_0_fun.9 = (f32[7,2,128,128]{3,2,1,0:T(8,128)S(1)}, f32[4,1,136,128]{3,2,1,0:T(8,128)S(1)}, f32[4,1,136,128]{3,2,1,0:T(8,128)S(1)}, f32[1,1,136,128]{3,2,...) custom-call(s32[7,3]{1,0:T(8,128)S(1)} %copy.103.off, ...), custom_call_target="tpu_custom_call" | custom-call | tf_op jit(solution)/shard_map/cond/branch_0_fun/pallas_call | solution.py:351
  37.7 1.7 %collective-permute-start.9 = (f32[4,1,136,128]{3,2,1,0:T(8,128)S(1)}, f32[4,1,136,128]{3,2,1,0:T(8,128)S(1)}, u32[]{:S(2)}, u32[]{:S(2)}) collective-permute-start(f32[4,1,136,128]{3,2,1,0:T(8,128)S(1)} %get-tuple-element.647), channel_id=1, source_target_pairs={{8,0},{16,8},{24,16},{0,24},{9,1},{17,9},{25,17},{1,25},{10,2},{18... | collective-permute-start | bytes 835592 | tf_op jit(solution)/shard_map/cond/branch_0_fun/ppermute | solution.py:373
  39.4 0.9 %collective-permute-start.10 = (f32[1,1,136,128]{3,2,1,0:T(8,128)S(1)}, f32[1,1,136,128]{3,2,1,0:T(8,128)S(1)}, u32[]{:S(2)}, u32[]{:S(2)}) collective-permute-start(f32[1,1,136,128]{3,2,1,0:T(8,128)S(1)} %get-tuple-element.648), channel_id=1, source_target_pairs={{0,1},{1,2},{2,3},{3,4},{4,5},{5,6},{6,7},{7,0},{8,9},{9,10},{10,1... | collective-permute-start | bytes 208904 | tf_op jit(solution)/shard_map/cond/branch_0_fun/ppermute | solution.py:374
  40.4 3.8 %collective-permute-start.11 = (f32[1,1,136,128]{3,2,1,0:T(8,128)S(1)}, f32[1,1,136,128]{3,2,1,0:T(8,128)S(1)}, u32[]{:S(2)}, u32[]{:S(2)}) collective-permute-start(f32[1,1,136,128]{3,2,1,0:T(8,128)S(1)} %get-tuple-element.648), channel_id=1, source_target_pairs={{1,0},{2,1},{3,2},{4,3},{5,4},{6,5},{7,6},{0,7},{9,8},{10,9},{11,1... | collective-permute-start | bytes 208904 | tf_op jit(solution)/shard_map/cond/branch_0_fun/ppermute | solution.py:375
  44.2 2.3 %collective-permute-done.10.col_low.after_col_low = f32[1,1,136,128]{3,2,1,0:T(8,128)S(1)} collective-permute-done((f32[1,1,136,128]{3,2,1,0:T(8,128)S(1)}, f32[1,1,136,128]{3,2,1,0:T(8,128)S(1)}, u32[]{:S(2)}, u32[]{:S(2)}) %collective-permute-start.10) | collective-permute-done | bytes 69664 | tf_op jit(solution)/shard_map/cond/branch_0_fun/ppermute | solution.py:374
  46.5 3.2 %branch_0_fun.11 = (f32[7,2,128,128]{3,2,1,0:T(8,128)S(1)}, f32[2,1,136,128]{3,2,1,0:T(8,128)S(1)}, f32[2,1,136,128]{3,2,1,0:T(8,128)S(1)}, f32[1,1,136,128]{3,2,1,0:T(8,128)S(1)}, f32[2,128,128]{2,1,0:T(8,128)S(1)}) custom-call(s32[7,3]{1,0:T(8,128)S(1)} %copy.103.off, s32[3]{0:T(128)S(1)} %copy-done.9, f32[7,2,128,128]{3,2,1,0:T(8,128)S(1)} %bitcast.637, ...), custom_call_target="tpu_custom_call" | custom-call | tf_op jit(solution)/shard_map/cond/branch_0_fun/pallas_call | solution.py:351
  49.9 1.7 %collective-permute-start.18 = (f32[2,1,136,128]{3,2,1,0:T(8,128)S(1)}, f32[2,1,136,128]{3,2,1,0:T(8,128)S(1)}, u32[]{:S(2)}, u32[]{:S(2)}) collective-permute-start(f32[2,1,136,128]{3,2,1,0:T(8,128)S(1)} %get-tuple-element.656), channel_id=1, source_target_pairs={{8,0},{16,8},{24,16},{0,24},{9,1},{17,9},{25,17},{1,25},{10,2},{18... | collective-permute-start | bytes 417800 | tf_op jit(solution)/shard_map/cond/branch_0_fun/ppermute | solution.py:373
  51.8 4.4 %collective-permute-start.20 = (f32[1,1,136,128]{3,2,1,0:T(8,128)S(1)}, f32[1,1,136,128]{3,2,1,0:T(8,128)S(1)}, u32[]{:S(2)}, u32[]{:S(2)}) collective-permute-start(f32[1,1,136,128]{3,2,1,0:T(8,128)S(1)} %get-tuple-element.657), channel_id=1, source_target_pairs={{1,0},{2,1},{3,2},{4,3},{5,4},{6,5},{7,6},{0,7},{9,8},{10,9},{11,1... | collective-permute-start | bytes 208904 | tf_op jit(solution)/shard_map/cond/branch_0_fun/ppermute | solution.py:375
  56.3 2.7 %branch_0_fun.10 = (f32[7,2,128,128]{3,2,1,0:T(8,128)}, f32[8,128]{1,0:T(8,128)S(1)}) custom-call(s32[7,3]{1,0:T(8,128)S(1)} %copy.103.off, s32[3]{0:T(128)S(1)} %copy-done.9, f32[7,2,128,128]{3,2,1,0:T(8,128)S(1)} %get-tuple-element.644.x.x_after, f32[2,128,128]{2,1,0:T(8,128)S(1)} %get-tuple-element.645.x_local, ...), custom_call_target="tpu_custom_call" | custom-call | tf_op jit(solution)/shard_map/cond/branch_0_fun/pallas_call | solution.py:351
  59.0 1.2 %collective-permute-done.12 = f32[8,128]{1,0:T(8,128)S(1)} collective-permute-done((f32[8,128]{1,0:T(8,128)S(1)}, f32[8,128]{1,0:T(8,128)S(1)}, u32[]{:S(2)}, u32[]{:S(2)}) %collective-permute-start.12) | collective-permute-done | bytes 4128 | tf_op jit(solution)/shard_map/cond/branch_0_fun/ppermute | solution.py:385
  60.7 3.0 %collective-permute-done.13 = f32[8,128]{1,0:T(8,128)S(1)} collective-permute-done((f32[8,128]{1,0:T(8,128)S(1)}, f32[8,128]{1,0:T(8,128)S(1)}, u32[]{:S(2)}, u32[]{:S(2)}) %collective-permute-start.13) | collective-permute-done | bytes 4128 | tf_op jit(solution)/shard_map/cond/branch_0_fun/ppermute | solution.py:385
  63.7 3.6 %collective-permute-done.14 = f32[8,128]{1,0:T(8,128)S(1)} collective-permute-done((f32[8,128]{1,0:T(8,128)S(1)}, f32[8,128]{1,0:T(8,128)S(1)}, u32[]{:S(2)}, u32[]{:S(2)}) %collective-permute-start.14) | collective-permute-done | bytes 4128 | tf_op jit(solution)/shard_map/cond/branch_0_fun/ppermute | solution.py:385
  67.4 3.6 %collective-permute-done.15 = f32[8,128]{1,0:T(8,128)S(1)} collective-permute-done((f32[8,128]{1,0:T(8,128)S(1)}, f32[8,128]{1,0:T(8,128)S(1)}, u32[]{:S(2)}, u32[]{:S(2)}) %collective-permute-start.15) | collective-permute-done | bytes 4128 | tf_op jit(solution)/shard_map/cond/branch_0_fun/ppermute | solution.py:385
  71.0 4.5 %collective-permute-done.16 = f32[8,128]{1,0:T(8,128)S(1)} collective-permute-done((f32[8,128]{1,0:T(8,128)S(1)}, f32[8,128]{1,0:T(8,128)S(1)}, u32[]{:S(2)}, u32[]{:S(2)}) %collective-permute-start.16) | collective-permute-done | bytes 4128 | tf_op jit(solution)/shard_map/cond/branch_0_fun/ppermute | solution.py:385
  75.5 3.5 %branch_0_fun.12 = (f32[7,2,128,128]{3,2,1,0:T(8,128)S(1)}, f32[2,1,136,128]{3,2,1,0:T(8,128)S(1)}, f32[2,1,136,128]{3,2,1,0:T(8,128)S(1)}, f32[1,1,136,128]{3,2,1,0:T(8,128)S(1)}, f32[2,128,128]{2,1,0:T(8,128)S(1)}) custom-call(s32[7,3]{1,0:T(8,128)S(1)} %copy.103.off, s32[3]{0:T(128)S(1)} %copy-done.9, f32[8,128]{1,0:T(8,128)S(1)} %add.728.sums, ...), custom_call_target="tpu_custom_call" | custom-call | tf_op jit(solution)/shard_map/cond/branch_0_fun/pallas_call | solution.py:351
  79.1 1.7 %collective-permute-start.22 = (f32[2,1,136,128]{3,2,1,0:T(8,128)S(1)}, f32[2,1,136,128]{3,2,1,0:T(8,128)S(1)}, u32[]{:S(2)}, u32[]{:S(2)}) collective-permute-start(f32[2,1,136,128]{3,2,1,0:T(8,128)S(1)} %get-tuple-element.661), channel_id=1, source_target_pairs={{8,0},{16,8},{24,16},{0,24},{9,1},{17,9},{25,17},{1,25},{10,2},{18... | collective-permute-start | bytes 417800 | tf_op jit(solution)/shard_map/cond/branch_0_fun/ppermute | solution.py:373
  80.8 4.7 %collective-permute-start.24 = (f32[1,1,136,128]{3,2,1,0:T(8,128)S(1)}, f32[1,1,136,128]{3,2,1,0:T(8,128)S(1)}, u32[]{:S(2)}, u32[]{:S(2)}) collective-permute-start(f32[1,1,136,128]{3,2,1,0:T(8,128)S(1)} %get-tuple-element.662), channel_id=1, source_target_pairs={{1,0},{2,1},{3,2},{4,3},{5,4},{6,5},{7,6},{0,7},{9,8},{10,9},{11,1... | collective-permute-start | bytes 208904 | tf_op jit(solution)/shard_map/cond/branch_0_fun/ppermute | solution.py:375
  86.1 1.7 %collective-permute-done.23.g_col_low = f32[1,1,136,128]{3,2,1,0:T(8,128)S(1)} collective-permute-done((f32[1,1,136,128]{3,2,1,0:T(8,128)S(1)}, f32[1,1,136,128]{3,2,1,0:T(8,128)S(1)}, u32[]{:S(2)}, u32[]{:S(2)}) %collective-permute-start.23) | collective-permute-done | bytes 69664 | tf_op jit(solution)/shard_map/cond/branch_0_fun/ppermute | solution.py:374
  87.8 3.1 %branch_0_fun.13 = f32[7,2,128,128]{3,2,1,0:T(8,128)} custom-call(s32[7,3]{1,0:T(8,128)S(1)} %copy.103.off, s32[3]{0:T(128)S(1)} %copy-done.9, f32[7,2,128,128]{3,2,1,0:T(8,128)S(1)} %get-tuple-element.658.g, f32[7,2,128,128]{3,2,1,0:T(8,128)S(1)} %bitcast.642, f32[2,128,128]{2,1,0:T(8,128)S(1)} %get-tuple-element.659.g_local, ...), custom_call_target="tpu_custom_call" | custom-call | tf_op jit(solution)/shard_map/cond/branch_0_fun/pallas_call | solution.py:351
  (44 shorter events, 5.7 us)
Async XLA Ops:
  5.9 27.9 %copy-start = (f32[1,1,7,2,128,128]{5,4,3,2,1,0:T(8,128)S(1)}, f32[1,1,7,2,128,128]{5,4,3,2,1,0:T(8,128)}, u32[]{:S(2)}) copy-start(f32[1,1,7,2,128,128]{5,4,3,2,1,0:T(8,128)} %get-tuple-element.634) | copy-start | bytes 2752516 | tf_op jit(solution)/shard_map/cond
  6.0 27.9 %copy-start.9 = (s32[3]{0:T(128)S(1)}, s32[3]{0:T(128)}, u32[]{:S(2)}) copy-start(s32[3]{0:T(128)} %get-tuple-element.632.branch) | copy-start | bytes 40 | tf_op jit(solution)/shard_map/cond
  9.1 12.9 %collective-permute-start = (f32[3,1,136,128]{3,2,1,0:T(8,128)S(1)}, f32[3,1,136,128]{3,2,1,0:T(8,128)S(1)}, u32[]{:S(2)}, u32[]{:S(2)}) collective-permute-start(f32[3,1,136,128]{3,2,1,0:T(8,128)S(1)} %get-tuple-element.636), channel_id=1, source_target_pairs={{0,8},{8,16},{16,24},{24,0},{1,9},{9,17},{17,25},{25,1},{2,10},{10... | collective-permute-start | bytes 626696 | tf_op jit(solution)/shard_map/cond/branch_0_fun/ppermute | solution.py:372
  9.6 12.4 %collective-permute-start.1 = (f32[3,1,136,128]{3,2,1,0:T(8,128)S(1)}, f32[3,1,136,128]{3,2,1,0:T(8,128)S(1)}, u32[]{:S(2)}, u32[]{:S(2)}) collective-permute-start(f32[3,1,136,128]{3,2,1,0:T(8,128)S(1)} %get-tuple-element.637), channel_id=1, source_target_pairs={{8,0},{16,8},{24,16},{0,24},{9,1},{17,9},{25,17},{1,25},{10,2},{18... | collective-permute-start | bytes 626696 | tf_op jit(solution)/shard_map/cond/branch_0_fun/ppermute | solution.py:373
  11.6 9.1 %collective-permute-start.2 = (f32[2,1,136,128]{3,2,1,0:T(8,128)S(1)}, f32[2,1,136,128]{3,2,1,0:T(8,128)S(1)}, u32[]{:S(2)}, u32[]{:S(2)}) collective-permute-start(f32[2,1,136,128]{3,2,1,0:T(8,128)S(1)} %get-tuple-element.638), channel_id=1, source_target_pairs={{0,1},{1,2},{2,3},{3,4},{4,5},{5,6},{6,7},{7,0},{8,9},{9,10},{10,1... | collective-permute-start | bytes 417800 | tf_op jit(solution)/shard_map/cond/branch_0_fun/ppermute | solution.py:374
  13.8 8.2 %collective-permute-start.3 = (f32[2,1,136,128]{3,2,1,0:T(8,128)S(1)}, f32[2,1,136,128]{3,2,1,0:T(8,128)S(1)}, u32[]{:S(2)}, u32[]{:S(2)}) collective-permute-start(f32[2,1,136,128]{3,2,1,0:T(8,128)S(1)} %get-tuple-element.638), channel_id=1, source_target_pairs={{1,0},{2,1},{3,2},{4,3},{5,4},{6,5},{7,6},{0,7},{9,8},{10,9},{11,1... | collective-permute-start | bytes 417800 | tf_op jit(solution)/shard_map/cond/branch_0_fun/ppermute | solution.py:375
  25.0 8.8 %collective-permute-start.4 = (f32[2,1,136,128]{3,2,1,0:T(8,128)S(1)}, f32[2,1,136,128]{3,2,1,0:T(8,128)S(1)}, u32[]{:S(2)}, u32[]{:S(2)}) collective-permute-start(f32[2,1,136,128]{3,2,1,0:T(8,128)S(1)} %get-tuple-element.641), channel_id=1, source_target_pairs={{0,8},{8,16},{16,24},{24,0},{1,9},{9,17},{17,25},{25,1},{2,10},{10... | collective-permute-start | bytes 417800 | tf_op jit(solution)/shard_map/cond/branch_0_fun/ppermute | solution.py:372
  25.1 8.7 %collective-permute-start.5 = (f32[2,1,136,128]{3,2,1,0:T(8,128)S(1)}, f32[2,1,136,128]{3,2,1,0:T(8,128)S(1)}, u32[]{:S(2)}, u32[]{:S(2)}) collective-permute-start(f32[2,1,136,128]{3,2,1,0:T(8,128)S(1)} %get-tuple-element.642), channel_id=1, source_target_pairs={{8,0},{16,8},{24,16},{0,24},{9,1},{17,9},{25,17},{1,25},{10,2},{18... | collective-permute-start | bytes 417800 | tf_op jit(solution)/shard_map/cond/branch_0_fun/ppermute | solution.py:373
  26.8 7.0 %collective-permute-start.6 = (f32[1,1,136,128]{3,2,1,0:T(8,128)S(1)}, f32[1,1,136,128]{3,2,1,0:T(8,128)S(1)}, u32[]{:S(2)}, u32[]{:S(2)}) collective-permute-start(f32[1,1,136,128]{3,2,1,0:T(8,128)S(1)} %get-tuple-element.643), channel_id=1, source_target_pairs={{0,1},{1,2},{2,3},{3,4},{4,5},{5,6},{6,7},{7,0},{8,9},{9,10},{10,1... | collective-permute-start | bytes 208904 | tf_op jit(solution)/shard_map/cond/branch_0_fun/ppermute | solution.py:374
  27.1 6.7 %collective-permute-start.7 = (f32[1,1,136,128]{3,2,1,0:T(8,128)S(1)}, f32[1,1,136,128]{3,2,1,0:T(8,128)S(1)}, u32[]{:S(2)}, u32[]{:S(2)}) collective-permute-start(f32[1,1,136,128]{3,2,1,0:T(8,128)S(1)} %get-tuple-element.643), channel_id=1, source_target_pairs={{1,0},{2,1},{3,2},{4,3},{5,4},{6,5},{7,6},{0,7},{9,8},{10,9},{11,1... | collective-permute-start | bytes 208904 | tf_op jit(solution)/shard_map/cond/branch_0_fun/ppermute | solution.py:375
  37.6 8.8 %collective-permute-start.8 = (f32[4,1,136,128]{3,2,1,0:T(8,128)S(1)}, f32[4,1,136,128]{3,2,1,0:T(8,128)S(1)}, u32[]{:S(2)}, u32[]{:S(2)}) collective-permute-start(f32[4,1,136,128]{3,2,1,0:T(8,128)S(1)} %get-tuple-element.646), channel_id=1, source_target_pairs={{0,8},{8,16},{16,24},{24,0},{1,9},{9,17},{17,25},{25,1},{2,10},{10... | collective-permute-start | bytes 835592 | tf_op jit(solution)/shard_map/cond/branch_0_fun/ppermute | solution.py:372
  37.7 8.7 %collective-permute-start.9 = (f32[4,1,136,128]{3,2,1,0:T(8,128)S(1)}, f32[4,1,136,128]{3,2,1,0:T(8,128)S(1)}, u32[]{:S(2)}, u32[]{:S(2)}) collective-permute-start(f32[4,1,136,128]{3,2,1,0:T(8,128)S(1)} %get-tuple-element.647), channel_id=1, source_target_pairs={{8,0},{16,8},{24,16},{0,24},{9,1},{17,9},{25,17},{1,25},{10,2},{18... | collective-permute-start | bytes 835592 | tf_op jit(solution)/shard_map/cond/branch_0_fun/ppermute | solution.py:373
  39.4 7.0 %collective-permute-start.10 = (f32[1,1,136,128]{3,2,1,0:T(8,128)S(1)}, f32[1,1,136,128]{3,2,1,0:T(8,128)S(1)}, u32[]{:S(2)}, u32[]{:S(2)}) collective-permute-start(f32[1,1,136,128]{3,2,1,0:T(8,128)S(1)} %get-tuple-element.648), channel_id=1, source_target_pairs={{0,1},{1,2},{2,3},{3,4},{4,5},{5,6},{6,7},{7,0},{8,9},{9,10},{10,1... | collective-permute-start | bytes 208904 | tf_op jit(solution)/shard_map/cond/branch_0_fun/ppermute | solution.py:374
  40.4 6.1 %collective-permute-start.11 = (f32[1,1,136,128]{3,2,1,0:T(8,128)S(1)}, f32[1,1,136,128]{3,2,1,0:T(8,128)S(1)}, u32[]{:S(2)}, u32[]{:S(2)}) collective-permute-start(f32[1,1,136,128]{3,2,1,0:T(8,128)S(1)} %get-tuple-element.648), channel_id=1, source_target_pairs={{1,0},{2,1},{3,2},{4,3},{5,4},{6,5},{7,6},{0,7},{9,8},{10,9},{11,1... | collective-permute-start | bytes 208904 | tf_op jit(solution)/shard_map/cond/branch_0_fun/ppermute | solution.py:375
  46.5 29.0 %copy-start.2 = (f32[1,1,7,2,128,128]{5,4,3,2,1,0:T(8,128)S(1)}, f32[1,1,7,2,128,128]{5,4,3,2,1,0:T(8,128)}, u32[]{:S(2)}) copy-start(f32[1,1,7,2,128,128]{5,4,3,2,1,0:T(8,128)} %get-tuple-element.633) | copy-start | bytes 2752516 | tf_op jit(solution)/shard_map/cond
  49.7 25.8 %collective-permute-start.17 = (f32[2,1,136,128]{3,2,1,0:T(8,128)S(1)}, f32[2,1,136,128]{3,2,1,0:T(8,128)S(1)}, u32[]{:S(2)}, u32[]{:S(2)}) collective-permute-start(f32[2,1,136,128]{3,2,1,0:T(8,128)S(1)} %get-tuple-element.655), channel_id=1, source_target_pairs={{0,8},{8,16},{16,24},{24,0},{1,9},{9,17},{17,25},{25,1},{2,10},{10... | collective-permute-start | bytes 417800 | tf_op jit(solution)/shard_map/cond/branch_0_fun/ppermute | solution.py:372
  49.9 25.6 %collective-permute-start.18 = (f32[2,1,136,128]{3,2,1,0:T(8,128)S(1)}, f32[2,1,136,128]{3,2,1,0:T(8,128)S(1)}, u32[]{:S(2)}, u32[]{:S(2)}) collective-permute-start(f32[2,1,136,128]{3,2,1,0:T(8,128)S(1)} %get-tuple-element.656), channel_id=1, source_target_pairs={{8,0},{16,8},{24,16},{0,24},{9,1},{17,9},{25,17},{1,25},{10,2},{18... | collective-permute-start | bytes 417800 | tf_op jit(solution)/shard_map/cond/branch_0_fun/ppermute | solution.py:373
  51.5 23.9 %collective-permute-start.19 = (f32[1,1,136,128]{3,2,1,0:T(8,128)S(1)}, f32[1,1,136,128]{3,2,1,0:T(8,128)S(1)}, u32[]{:S(2)}, u32[]{:S(2)}) collective-permute-start(f32[1,1,136,128]{3,2,1,0:T(8,128)S(1)} %get-tuple-element.657), channel_id=1, source_target_pairs={{0,1},{1,2},{2,3},{3,4},{4,5},{5,6},{6,7},{7,0},{8,9},{9,10},{10,1... | collective-permute-start | bytes 208904 | tf_op jit(solution)/shard_map/cond/branch_0_fun/ppermute | solution.py:374
  51.8 23.6 %collective-permute-start.20 = (f32[1,1,136,128]{3,2,1,0:T(8,128)S(1)}, f32[1,1,136,128]{3,2,1,0:T(8,128)S(1)}, u32[]{:S(2)}, u32[]{:S(2)}) collective-permute-start(f32[1,1,136,128]{3,2,1,0:T(8,128)S(1)} %get-tuple-element.657), channel_id=1, source_target_pairs={{1,0},{2,1},{3,2},{4,3},{5,4},{6,5},{7,6},{0,7},{9,8},{10,9},{11,1... | collective-permute-start | bytes 208904 | tf_op jit(solution)/shard_map/cond/branch_0_fun/ppermute | solution.py:375
  59.0 1.2 %collective-permute-start.12 = (f32[8,128]{1,0:T(8,128)S(1)}, f32[8,128]{1,0:T(8,128)S(1)}, u32[]{:S(2)}, u32[]{:S(2)}) collective-permute-start(f32[8,128]{1,0:T(8,128)S(1)} %get-tuple-element.650), channel_id=1, source_target_pairs={{0,8},{8,0},{16,24},{24,16},{1,9},{9,1},{17,25},{25,17},{2,10},{10... | collective-permute-start | bytes 12296 | tf_op jit(solution)/shard_map/cond/branch_0_fun/ppermute | solution.py:385
  60.1 3.6 %collective-permute-start.13 = (f32[8,128]{1,0:T(8,128)S(1)}, f32[8,128]{1,0:T(8,128)S(1)}, u32[]{:S(2)}, u32[]{:S(2)}) collective-permute-start(f32[8,128]{1,0:T(8,128)S(1)} %add.724), channel_id=1, source_target_pairs={{0,16},{8,24},{16,0},{24,8},{1,17},{9,25},{17,1},{25,9},{2,18},{10... | collective-permute-start | bytes 12296 | tf_op jit(solution)/shard_map/cond/branch_0_fun/ppermute | solution.py:385
  63.7 3.6 %collective-permute-start.14 = (f32[8,128]{1,0:T(8,128)S(1)}, f32[8,128]{1,0:T(8,128)S(1)}, u32[]{:S(2)}, u32[]{:S(2)}) collective-permute-start(f32[8,128]{1,0:T(8,128)S(1)} %add.725), channel_id=1, source_target_pairs={{0,1},{1,0},{2,3},{3,2},{4,5},{5,4},{6,7},{7,6},{8,9},{9,8},{10,11... | collective-permute-start | bytes 12296 | tf_op jit(solution)/shard_map/cond/branch_0_fun/ppermute | solution.py:385
  67.3 3.6 %collective-permute-start.15 = (f32[8,128]{1,0:T(8,128)S(1)}, f32[8,128]{1,0:T(8,128)S(1)}, u32[]{:S(2)}, u32[]{:S(2)}) collective-permute-start(f32[8,128]{1,0:T(8,128)S(1)} %add.726), channel_id=1, source_target_pairs={{0,2},{1,3},{2,0},{3,1},{4,6},{5,7},{6,4},{7,5},{8,10},{9,11},{10,... | collective-permute-start | bytes 12296 | tf_op jit(solution)/shard_map/cond/branch_0_fun/ppermute | solution.py:385
  71.0 4.5 %collective-permute-start.16 = (f32[8,128]{1,0:T(8,128)S(1)}, f32[8,128]{1,0:T(8,128)S(1)}, u32[]{:S(2)}, u32[]{:S(2)}) collective-permute-start(f32[8,128]{1,0:T(8,128)S(1)} %add.727), channel_id=1, source_target_pairs={{0,4},{1,5},{2,6},{3,7},{4,0},{5,1},{6,2},{7,3},{8,12},{9,13},{10,... | collective-permute-start | bytes 12296 | tf_op jit(solution)/shard_map/cond/branch_0_fun/ppermute | solution.py:385
  79.0 8.8 %collective-permute-start.21 = (f32[2,1,136,128]{3,2,1,0:T(8,128)S(1)}, f32[2,1,136,128]{3,2,1,0:T(8,128)S(1)}, u32[]{:S(2)}, u32[]{:S(2)}) collective-permute-start(f32[2,1,136,128]{3,2,1,0:T(8,128)S(1)} %get-tuple-element.660), channel_id=1, source_target_pairs={{0,8},{8,16},{16,24},{24,0},{1,9},{9,17},{17,25},{25,1},{2,10},{10... | collective-permute-start | bytes 417800 | tf_op jit(solution)/shard_map/cond/branch_0_fun/ppermute | solution.py:372
  79.1 8.7 %collective-permute-start.22 = (f32[2,1,136,128]{3,2,1,0:T(8,128)S(1)}, f32[2,1,136,128]{3,2,1,0:T(8,128)S(1)}, u32[]{:S(2)}, u32[]{:S(2)}) collective-permute-start(f32[2,1,136,128]{3,2,1,0:T(8,128)S(1)} %get-tuple-element.661), channel_id=1, source_target_pairs={{8,0},{16,8},{24,16},{0,24},{9,1},{17,9},{25,17},{1,25},{10,2},{18... | collective-permute-start | bytes 417800 | tf_op jit(solution)/shard_map/cond/branch_0_fun/ppermute | solution.py:373
  80.8 7.0 %collective-permute-start.23 = (f32[1,1,136,128]{3,2,1,0:T(8,128)S(1)}, f32[1,1,136,128]{3,2,1,0:T(8,128)S(1)}, u32[]{:S(2)}, u32[]{:S(2)}) collective-permute-start(f32[1,1,136,128]{3,2,1,0:T(8,128)S(1)} %get-tuple-element.662), channel_id=1, source_target_pairs={{0,1},{1,2},{2,3},{3,4},{4,5},{5,6},{6,7},{7,0},{8,9},{9,10},{10,1... | collective-permute-start | bytes 208904 | tf_op jit(solution)/shard_map/cond/branch_0_fun/ppermute | solution.py:374
  80.8 7.0 %collective-permute-start.24 = (f32[1,1,136,128]{3,2,1,0:T(8,128)S(1)}, f32[1,1,136,128]{3,2,1,0:T(8,128)S(1)}, u32[]{:S(2)}, u32[]{:S(2)}) collective-permute-start(f32[1,1,136,128]{3,2,1,0:T(8,128)S(1)} %get-tuple-element.662), channel_id=1, source_target_pairs={{1,0},{2,1},{3,2},{4,3},{5,4},{6,5},{7,6},{0,7},{9,8},{10,9},{11,1... | collective-permute-start | bytes 208904 | tf_op jit(solution)/shard_map/cond/branch_0_fun/ppermute | solution.py:375
